TPU v7x, 256 devices: a whole 4x4x8 slice. The times are simulated.
256 devices in a mesh: dp: 16 (over x, y), expert: 16 (over z, core).
Axes of the slice: x: 4, y: 4, z: 8, core: 2. Of those that a mesh axis runs over, the one named last changes fastest.
Arguments:
- tokens: bfloat16 [32768, 7168], P(('dp', 'expert')), may hold values from -6 to 6
- tangent: bfloat16 [32768, 7168], P(('dp', 'expert')), may hold values from -6 to 6
- expert_ids: int32 [32768, 8], P(('dp', 'expert')), may hold values from 0 to 255, as said below
- gates: bfloat16 [32768, 8], P(('dp', 'expert')), may hold values from 0.049804688 to 0.5
- precision: float32 [7168], replicated, may hold values from 1 to 10
- gate_weight: bfloat16 [16, 1792, 2048], P('expert', None, 'dp'), may hold values from -0.0625 to 0.0625
- up_weight: bfloat16 [16, 1792, 2048], P('expert', None, 'dp'), may hold values from -0.0625 to 0.0625
- down_weight: bfloat16 [16, 1792, 2048], P('expert', None, 'dp'), may hold values from -0.125 to 0.125
Outputs:
- grad_gate: bfloat16 [16, 1792, 2048], P('expert', None, 'dp')
- grad_up: bfloat16 [16, 1792, 2048], P('expert', None, 'dp')
- grad_down: bfloat16 [16, 1792, 2048], P('expert', None, 'dp')
Inputs may be any that keep to these rules, and one draw needn't show every extreme that they name: `expert_ids`: each row names 8 different experts. The rows of one device name each expert below 4 at least once and at most 4 times, and in every draw the rows of every device name one such expert exactly 4 times.
All inputs are finite; a program needn't handle non-finite values.
Results may differ from a plain program's by a relative error of at most 0.024.
Values may be sent and summed in bfloat16 or wider, within the bound.
No kernel may reach another device: no remote copies, remote signals or barrier semaphores. Data moves between devices by JAX's collectives and lax.ppermute only.
A program may use at most 128 MiB of HBM per device.

v0:
```python
import jax
import jax.numpy as jnp
from jax import lax
from jax.sharding import PartitionSpec as P

EXPERTS = 4
CAP = 4


def partner_2(value, axis, stride):
    mask = 2**stride
    pairs = [(source, source ^ mask) for source in range(lax.axis_size(axis))]
    return lax.ppermute(value, axis, pairs)


def silu_parts(preact):
    sigma_val = jax.nn.sigmoid(preact)
    return (preact * sigma_val, sigma_val * (1.0 + preact * (1.0 - sigma_val)))


def body(tokens, tangent, expert_ids, gates, precision, gate_weight, up_weight, down_weight):
    owner_count = lax.axis_size("expert")
    tok_rows, features = tokens.shape
    picks_per_row = expert_ids.shape[1]
    replicas = owner_count // EXPERTS
    levels = replicas.bit_length() - 1
    per_peer = CAP // replicas
    slot_count = owner_count * per_peer
    flat_ids = expert_ids.reshape(tok_rows * picks_per_row)
    onehot = (flat_ids[:, None] == jnp.arange(EXPERTS, dtype=jnp.int32)[None, :]).astype(jnp.int32)
    before = jnp.cumsum(onehot, axis=0) - onehot
    slot_of = jnp.sum(before * onehot, axis=1)
    inside = jnp.sum(onehot, axis=1)
    target = (flat_ids * replicas + slot_of % replicas) * per_peer + slot_of // replicas
    target = jnp.where(inside > 0, target, -1).reshape(tok_rows, picks_per_row)
    matches = target[:, :, None] == jnp.arange(slot_count, dtype=jnp.int32)[None, None, :]
    placed = jnp.sum(jnp.where(matches, gates[:, :, None], jnp.zeros((), jnp.bfloat16)), axis=1)
    position = lax.axis_index("expert")
    weights = jnp.stack([gate_weight[0], up_weight[0], down_weight[0]])
    for bit_index in range(levels):
        partner = partner_2(weights, "expert", bit_index)
        upper_half = position >> bit_index & 1 == 1
        weights = jnp.where(
            upper_half,
            jnp.concatenate([partner, weights], 1),
            jnp.concatenate([weights, partner], 1),
        )
    w_gate, w_up, w_down = (weights[0], weights[1], weights[2])

    def deliver(stacked, scaled):
        selector = (placed > 0).astype(jnp.bfloat16)
        chosen = jnp.einsum("tc,ktd->kcd", selector, stacked, preferred_element_type=jnp.float32)
        if scaled:
            weights_here = jnp.sum(placed.astype(jnp.float32), axis=0)
            chosen = chosen * weights_here[None, :, None]
        exchanged = lax.all_to_all(
            chosen.astype(jnp.bfloat16), "expert", split_axis=1, concat_axis=1, tiled=True
        )
        return lax.all_gather(exchanged, "dp", axis=1, tiled=True)

    routed = deliver(jnp.stack([tokens, tangent]), False)
    routed_total = routed.shape[1]
    both_rows = routed.reshape(2 * routed_total, features)
    gate_pre = jnp.dot(both_rows, w_gate, preferred_element_type=jnp.float32).reshape(
        2, routed_total, -1
    )
    up_pre = jnp.dot(both_rows, w_up, preferred_element_type=jnp.float32).reshape(
        2, routed_total, -1
    )
    activated, derivative = silu_parts(gate_pre[0])
    up_main = up_pre[0]
    hidden_out = (activated * up_main).astype(jnp.bfloat16)
    hidden_tan = (derivative * gate_pre[1] * up_main + activated * up_pre[1]).astype(jnp.bfloat16)
    product = lax.dot_general(
        hidden_tan, w_down, (((1,), (1,)), ((), ())), preferred_element_type=jnp.float32
    )
    product = lax.optimization_barrier(product.astype(jnp.bfloat16))
    summed = lax.psum_scatter(
        product.astype(jnp.float32).astype(jnp.bfloat16), "dp", scatter_dimension=0, tiled=True
    )
    returned = lax.all_to_all(summed, "expert", split_axis=0, concat_axis=0, tiled=True)
    combined = jnp.dot(
        placed.astype(jnp.float32), returned.astype(jnp.float32), precision=lax.Precision.HIGHEST
    )
    cotangent = (precision[None, :] * combined).astype(jnp.bfloat16)
    cot_rows = deliver(cotangent[None], True)[0]
    back_grad = jnp.dot(cot_rows, w_down, preferred_element_type=jnp.float32)
    gate_cot = (back_grad * up_main * derivative).astype(jnp.bfloat16)
    up_cot = (back_grad * activated).astype(jnp.bfloat16)
    x_rows = routed[0]
    contract = (((0,), (0,)), ((), ()))
    partials = jnp.stack(
        [
            lax.dot_general(x_rows, gate_cot, contract, preferred_element_type=jnp.float32),
            lax.dot_general(x_rows, up_cot, contract, preferred_element_type=jnp.float32),
            lax.dot_general(cot_rows, hidden_out, contract, preferred_element_type=jnp.float32),
        ]
    )
    for bit_index in reversed(range(levels)):
        half_width = partials.shape[1] // 2
        upper_half = position >> bit_index & 1 == 1
        retained = jnp.where(upper_half, partials[:, half_width:], partials[:, :half_width])
        outgoing = jnp.where(upper_half, partials[:, :half_width], partials[:, half_width:])
        partials = retained + partner_2(outgoing.astype(jnp.bfloat16), "expert", bit_index).astype(
            outgoing.dtype
        )
    grad_gate, grad_up, grad_down = (partials[0], partials[1], partials[2])
    return (
        grad_gate.astype(jnp.bfloat16)[None],
        grad_up.astype(jnp.bfloat16)[None],
        grad_down.astype(jnp.bfloat16)[None],
    )


def solution(mesh):
    in_specs = (
        P(("dp", "expert"), None),
        P(("dp", "expert"), None),
        P(("dp", "expert"), None),
        P(("dp", "expert"), None),
        P(),
        P("expert", None, "dp"),
        P("expert", None, "dp"),
        P("expert", None, "dp"),
    )
    out_specs = (P("expert", None, "dp"), P("expert", None, "dp"), P("expert", None, "dp"))
    return jax.shard_map(body, mesh=mesh, in_specs=in_specs, out_specs=out_specs, check_vma=False)
```

profile of v0, /device:TPU:1, one launch (start us, length us, event | category | flops | bytes accessed | tf_op | source)
XLA Modules:
  0.0 401.3 jit_solution(1602465592122075495)
XLA Ops:
  8.2 1.1 reduce-window.6
  11.9 2.8 fusion.1
  15.1 25.7 %all_to_all.22 = bf16[2,16,7168]{2,0,1:T(2,128)(2,1)S(1)} all-to-all(bf16[2,16,7168]{2,0,1:T(2,128)(2,1)S(1)} %copy.49), channel_id=1, replica_groups=mesh['dp'=16,'expert'=16] {'expert'}, dimensions={1} | all-to-all | bytes 917504 | tf_op jit(solution)/shard_map/all_to_all | solution.py:56
  42.1 1.0 copy-done.1
  43.2 2.2 collective-permute-done
  45.4 3.4 maximum_select_fusion.1
  48.9 61.2 %collective-permute-done.1 = bf16[3,3584,128]{2,1,0:T(8,128)(2,1)} collective-permute-done((bf16[3,3584,128]{2,1,0:T(8,128)(2,1)S(1)}, bf16[3,3584,128]{2,1,0:T(8,128)(2,1)}, u32[]{:S(2)}, u32[]{:S(2)}) %collective-permute-start.1) | collective-permute-done | bytes 2752544 | tf_op jit(solution)/shard_map/ppermute | solution.py:13
  110.1 7.0 %maximum_select_fusion = bf16[3,7168,128]{2,1,0:T(8,128)(2,1)} fusion(bf16[3,3584,128]{2,1,0:T(8,128)(2,1)S(1)} %maximum_select_fusion.1, bf16[3,3584,128]{2,1,0:T(8,128)(2,1)} %collective-permute-done.1, pred[]{:T(512)S(6)} %eq.49), kind=kLoop, calls=%fused_computation.13 | loop fusion | flops 24772608 | bytes 11010049 | tf_op jit(solution)/shard_map/jit(_where)/select_n | solution.py:43
  117.1 5.8 %fusion.12 = f32[512,128]{1,0:T(8,128)S(1)} fusion(bf16[512,7168]{1,0:T(8,128)(2,1)} %bitcast.66, bf16[3,7168,128]{2,1,0:T(8,128)(2,1)} %maximum_select_fusion), kind=kOutput, calls=%fused_computation.30 | convolution fusion | flops 939524096 | bytes 9437184 | tf_op jit(solution)/shard_map/dot_general | solution.py:64
  122.9 3.6 fusion.11
  126.5 4.4 %convolution_convert_fusion = bf16[256,7168]{1,0:T(8,128)(2,1)} fusion(bf16[3,7168,128]{2,1,0:T(8,128)(2,1)} %maximum_select_fusion, f32[512,128]{1,0:T(8,128)S(1)} %fusion.11, f32[512,128]{1,0:T(8,128)S(1)} %fusion.12), kind=kOutput, calls=%fused_computation.1 | convolution fusion | flops 472023040 | bytes 6029312 | tf_op jit(solution)/shard_map/dot_general | solution.py:74
  131.0 77.2 %reduce-scatter.2.cloned.1.call-done = bf16[16,7168]{1,0:T(8,128)(2,1)} async-done(((bf16[256,7168]{1,0:T(8,128)(2,1)}), bf16[16,7168]{1,0:T(8,128)(2,1)}) %reduce-scatter.2.cloned.1.call-update) | async-done | bytes 229392 | tf_op jit(solution)/shard_map/reduce_scatter | solution.py:78
  208.7 1.7 reduce.3
  210.4 0.8 reshape.96
  211.2 9.4 %all-to-all-start.1 = ((bf16[16,2,3584]{2,1,0:T(2,128)(2,1)}), bf16[16,2,3584]{2,1,0:T(2,128)(2,1)S(1)}, u32[]{:S(2)}, u32[]{:S(2)}) async-start(bf16[16,2,3584]{2,1,0:T(2,128)(2,1)} %reshape.96), calls=%async_computation.2 | async-start | bytes 458752 | tf_op jit(solution)/shard_map/all_to_all | solution.py:81
  220.9 10.7 %all-to-all-done.1 = bf16[16,2,3584]{2,1,0:T(2,128)(2,1)S(1)} async-done(((bf16[16,2,3584]{2,1,0:T(2,128)(2,1)}), bf16[16,2,3584]{2,1,0:T(2,128)(2,1)S(1)}, u32[]{:S(2)}, u32[]{:S(2)}) %all-to-all-start.1) | async-done | bytes 229408 | tf_op jit(solution)/shard_map/all_to_all | solution.py:81
  233.2 2.0 reduce.4
  235.4 13.7 %all_to_all.23 = bf16[16,2,3584]{2,1,0:T(2,128)(2,1)S(1)} all-to-all(bf16[16,2,3584]{2,1,0:T(2,128)(2,1)S(1)} %reshape.98), channel_id=1, replica_groups=mesh['dp'=16,'expert'=16] {'expert'}, dimensions={0} | all-to-all | bytes 458752 | tf_op jit(solution)/shard_map/all_to_all | solution.py:56
  250.0 48.9 %all-gather.5.cloned.1.call-done = bf16[1,256,7168]{2,1,0:T(8,128)(2,1)} async-done(((bf16[1,16,7168]{2,1,0:T(8,128)(2,1)}), bf16[1,256,7168]{2,1,0:T(8,128)(2,1)}) %all-gather.5.cloned.1.call-update) | async-done | bytes 3670032 | tf_op jit(solution)/shard_map/all_gather | solution.py:59
  298.9 3.9 fusion.9
  302.8 5.3 %convolution_bitcast_fusion = f32[1,7168,128]{2,1,0:T(8,128)} fusion(bf16[1,256,7168]{2,1,0:T(8,128)(2,1)} %all-gather.5.cloned.1.call-done, f32[512,128]{1,0:T(8,128)S(1)} %fusion.11, f32[512,128]{1,0:T(8,128)S(1)} %fusion.12), kind=kOutput, calls=%fused_computation.2 | convolution fusion | flops 469958656 | bytes 7602176 | tf_op jit(solution)/shard_map/dot_general | solution.py:96
  308.1 3.0 convolution_bitcast_fusion.2
  311.1 3.0 convolution_bitcast_fusion.1
  314.1 4.9 %pad_maximum_fusion = f32[3,7168,128]{2,1,0:T(8,128)S(1)} fusion(f32[1,7168,128]{2,1,0:T(8,128)} %convolution_bitcast_fusion, f32[1,7168,128]{2,1,0:T(8,128)} %convolution_bitcast_fusion.1, f32[1,7168,128]{2,1,0:T(8,128)} %convolution_bitcast_fusion.2), kind=kLoop, calls=%fused_computation | loop fusion | flops 5505024 | bytes 22020096 | tf_op jit(solution)/shard_map/stack | solution.py:92
  319.5 1.4 collective-permute-start.2
  320.8 58.8 %collective-permute-done.2 = bf16[3,3584,128]{2,1,0:T(8,128)(2,1)S(1)} collective-permute-done((bf16[3,3584,128]{2,1,0:T(8,128)(2,1)S(1)}, bf16[3,3584,128]{2,1,0:T(8,128)(2,1)S(1)}, u32[]{:S(2)}, u32[]{:S(2)}) %collective-permute-start.2) | collective-permute-done | bytes 2752544 | tf_op jit(solution)/shard_map/ppermute | solution.py:13
  379.7 3.3 convert_add_fusion
  382.9 2.9 select_convert_fusion.1
  385.8 2.1 collective-permute-start.3
  387.9 2.8 collective-permute-done.3
  390.6 3.0 add_convert_fusion
  393.7 1.1 fusion.38
  (59 shorter events, 9.2 us)
Async XLA Ops:
  7.2 110.0 %all-gather.3.cloned.1.call-start = ((), (), s32[]{:S(2)}) async-start(), calls=%async_computation.4 | async-start | bytes 7798784 | tf_op jit(solution)/shard_map/all_gather | solution.py:59
  11.8 30.0 %copy-start.2 = (bf16[1,1792,128]{2,1,0:T(8,128)(2,1)S(1)}, bf16[1,1792,128]{2,1,0:T(8,128)(2,1)}, u32[]{:S(2)}) copy-start(bf16[1,1792,128]{2,1,0:T(8,128)(2,1)} %param.13) | copy-start | bytes 1376260
  11.9 30.0 %copy-start.3 = (bf16[1,1792,128]{2,1,0:T(8,128)(2,1)S(1)}, bf16[1,1792,128]{2,1,0:T(8,128)(2,1)}, u32[]{:S(2)}) copy-start(bf16[1,1792,128]{2,1,0:T(8,128)(2,1)} %param.14) | copy-start | bytes 1376260
  14.6 27.3 %copy-start.4 = (bf16[1,1792,128]{2,1,0:T(8,128)(2,1)S(1)}, bf16[1,1792,128]{2,1,0:T(8,128)(2,1)}, u32[]{:S(2)}) copy-start(bf16[1,1792,128]{2,1,0:T(8,128)(2,1)} %param.15) | copy-start | bytes 1376260
  41.8 166.4 %reduce-scatter.2.cloned.1.call-start = ((), (), s32[]{:S(2)}) async-start(), calls=%async_computation.5 | async-start | bytes 3899392 | tf_op jit(solution)/shard_map/reduce_scatter | solution.py:78
  42.0 1.1 copy-start.1
  42.0 3.3 collective-permute-start
  48.8 61.3 %collective-permute-start.1 = (bf16[3,3584,128]{2,1,0:T(8,128)(2,1)S(1)}, bf16[3,3584,128]{2,1,0:T(8,128)(2,1)}, u32[]{:S(2)}, u32[]{:S(2)}) collective-permute-start(bf16[3,3584,128]{2,1,0:T(8,128)(2,1)S(1)} %maximum_select_fusion.1), channel_id=1, source_target_pairs={{0,2},{1,3},{2,0},{3,1},{4,6},{5,7},{6,4},{7,5},{8,10},{9,11},{10,... | collective-permute-start | bytes 8257544 | tf_op jit(solution)/shard_map/ppermute | solution.py:13
  117.1 5.8 %copy-start = (bf16[2,256,7168]{2,1,0:T(8,128)(2,1)S(1)}, bf16[2,256,7168]{2,1,0:T(8,128)(2,1)}, u32[]{:S(2)}) copy-start(bf16[2,256,7168]{2,1,0:T(8,128)(2,1)} %all-gather.3.cloned.1.call-done) | copy-start | bytes 22020100
  130.9 100.9 %copy-start.5 = (f32[7168]{0:T(1024)S(1)}, f32[7168]{0:T(1024)}, u32[]{:S(2)}) copy-start(f32[7168]{0:T(1024)} %param.12) | copy-start | bytes 86020
  211.2 20.4 %all-to-all-start.1 = ((bf16[16,2,3584]{2,1,0:T(2,128)(2,1)}), bf16[16,2,3584]{2,1,0:T(2,128)(2,1)S(1)}, u32[]{:S(2)}, u32[]{:S(2)}) async-start(bf16[16,2,3584]{2,1,0:T(2,128)(2,1)} %reshape.96), calls=%async_computation.2 | async-start | bytes 458752 | tf_op jit(solution)/shard_map/all_to_all | solution.py:81
  220.6 78.3 %all-gather.5.cloned.1.call-start = ((), (), s32[]{:S(2)}) async-start(), calls=%async_computation.6 | async-start | bytes 3899392 | tf_op jit(solution)/shard_map/all_gather | solution.py:59
  298.9 9.1 %slice-start = ((s8[7340032]{0:T(1024)(128)(4,1)}), s8[4194304]{0:T(1024)(128)(4,1)S(1)}, s32[]{:S(2)}) async-start(s8[7340032]{0:T(1024)(128)(4,1)} %bitcast.68), calls=%async_computation.7 | async-start | bytes 8388608
  302.8 5.3 %slice-start.1 = ((s8[7340032]{0:T(1024)(128)(4,1)}), s8[3145728]{0:T(1024)(128)(4,1)S(1)}, s32[]{:S(2)}) async-start(s8[7340032]{0:T(1024)(128)(4,1)} %bitcast.68), calls=%async_computation.8 | async-start | bytes 6291456
  319.5 60.2 %collective-permute-start.2 = (bf16[3,3584,128]{2,1,0:T(8,128)(2,1)S(1)}, bf16[3,3584,128]{2,1,0:T(8,128)(2,1)S(1)}, u32[]{:S(2)}, u32[]{:S(2)}) collective-permute-start(bf16[3,3584,128]{2,1,0:T(8,128)(2,1)S(1)} %select_convert_fusion), channel_id=1, source_target_pairs={{0,2},{1,3},{2,0},{3,1},{4,6},{5,7},{6,4},{7,5},{8,10},{9,11},{10,... | collective-permute-start | bytes 8257544 | tf_op jit(solution)/shard_map/ppermute | solution.py:13
  385.8 4.8 %collective-permute-start.3 = (bf16[3,1792,128]{2,1,0:T(8,128)(2,1)S(1)}, bf16[3,1792,128]{2,1,0:T(8,128)(2,1)S(1)}, u32[]{:S(2)}, u32[]{:S(2)}) collective-permute-start(bf16[3,1792,128]{2,1,0:T(8,128)(2,1)S(1)} %select_convert_fusion.1), channel_id=1, source_target_pairs={{0,1},{1,0},{2,3},{3,2},{4,5},{5,4},{6,7},{7,6},{8,9},{9,8},{10,11... | collective-permute-start | bytes 4128776 | tf_op jit(solution)/shard_map/ppermute | solution.py:13
Sparse Core Ops, SparseCore 0:
  41.9 67.8 all-gather.2
  131.1 77.0 reduce-scatter.1
  250.1 48.7 all-gather.4
where the time goes:
time: 402 us; the launch traced here: 401 us
  waiting for transfers between devices  262 us (65%)
  blocking collectives  39.4 us (10%)
  matrix products  32.7 us (8%)
  other arithmetic  31.7 us (8%)
  between operations  14 us (3%)
  starting transfers between devices  13.3 us (3%)
  local copies, waits for them, and re-layouts  8.24 us (2%)
    ppermute x4, waiting for transfers between devices, partner_2(): return lax.ppermute(value, axis, pairs)  125 us
    reduce_scatter x1, waiting for transfers between devices, body(): lax.psum_scatter(product.astype(jnp.float32).astype(jnp.bfloat16), 'dp',...  77.2 us
    all_gather x2, waiting for transfers between devices, deliver(): return lax.all_gather(exchanged, 'dp', axis=1, tiled=True)  48.9 us
    all_to_all x2, blocking collectives, deliver(): lax.all_to_all(chosen.astype(jnp.bfloat16), 'expert', split_axis=1, conca...  39.4 us
    all_to_all x1, waiting for transfers between devices, body(): lax.all_to_all(summed, 'expert', split_axis=0, concat_axis=0, tiled=True)  10.7 us
    select_n x2, other arithmetic, body(): jnp.where(upper_half, jnp.concatenate([partner, weights], 1), jnp.concate...  10.4 us
    all_to_all x1, starting transfers between devices, body(): lax.all_to_all(summed, 'expert', split_axis=0, concat_axis=0, tiled=True)  9.39 us
  transfers between devices with their start and end apart: 8, of which 7 were waited for; matrix products, arithmetic and copies ran while one was open for 3% of the time, Pallas kernels for 0%

commit v1 on v0

v1 whole, which is shorter than its diff:
```python
import jax
import jax.numpy as jnp
from jax import lax
from jax.sharding import Mesh, PartitionSpec as P

EXPERTS = 4
CAP = 4
NX, NY, NZ, NC = 4, 4, 8, 2
RING = 4
BF16 = jnp.bfloat16
F32 = jnp.float32
ALL = ("x", "y", "z", "c")


def sigmoid_parts(preact):
    sigma_val = jax.nn.sigmoid(preact)
    return preact * sigma_val, sigma_val * (1.0 + preact * (1.0 - sigma_val))


def plane_shift(value, step, first):
    pairs = []
    for x in range(NX):
        for y in range(NY):
            for c in range(NC):
                if (c == 0) == first:
                    to = ((x + step) % NX, y, c)
                else:
                    to = (x, (y + step) % NY, c)
                pairs.append(((x * NY + y) * NC + c, (to[0] * NY + to[1]) * NC + to[2]))
    return lax.ppermute(value, ("x", "y", "c"), pairs)


def gather_phase(value, first):
    return [value] + [plane_shift(value, step, first) for step in (1, 2, 3)]


def plane_gather(value):
    got = lax.optimization_barrier(tuple(gather_phase(value, True)))
    return gather_phase(jnp.stack(got), False)


def scatter_phase(pieces, first):
    moved = [pieces[0]] + [plane_shift(pieces[step], -step, first) for step in (1, 2, 3)]
    moved = lax.optimization_barrier(tuple(moved))
    total = moved[0].astype(F32)
    for piece in moved[1:]:
        total = total + piece.astype(F32)
    return total.astype(BF16)


def core_swap(value):
    return lax.ppermute(value, "c", [(0, 1), (1, 0)])


def z_swap(value):
    return lax.ppermute(value, "z", [(z, z ^ 1) for z in range(NZ)])


def core_sum(value):
    other = core_swap(value)
    return value + jnp.swapaxes(other, 0, 1)


def body(tokens, tangent, expert_ids, gates, precision, gate_weight, up_weight, down_weight):
    tok_rows, features = tokens.shape
    block = gate_weight.shape[1]
    hidden = gate_weight.shape[2]
    half = 2 * block
    core = lax.axis_index("c")
    parity = lax.axis_index("z") % 2

    onehot = expert_ids[:, :, None] == jnp.arange(EXPERTS, dtype=jnp.int32)[None, None, :]
    has = jnp.any(onehot, axis=1)
    gate = jnp.sum(jnp.where(onehot, gates[:, :, None], jnp.zeros((), BF16)), axis=1)
    order = jnp.arange(tok_rows, dtype=jnp.int32)
    earlier = (order[None, :] < order[:, None]).astype(BF16)
    before = jnp.dot(earlier, has.astype(BF16), preferred_element_type=F32)
    slots = jnp.arange(CAP, dtype=F32)
    hit = has[:, :, None] & (before[:, :, None] == slots[None, None, :])
    selector = hit.astype(BF16).reshape(tok_rows, EXPERTS * CAP)
    placed = jnp.where(hit, gate[:, :, None], jnp.zeros((), BF16)).reshape(tok_rows, EXPERTS * CAP)

    both = jnp.stack([tokens, tangent])
    chosen = jnp.einsum("tr,ktd->krd", selector, both, preferred_element_type=F32).astype(BF16)
    chosen = chosen.reshape(2, NZ, 2, 2, NC, block)
    chosen = jnp.transpose(chosen, (1, 4, 0, 2, 3, 5)).reshape(NZ * NC * 4, half)
    sent = lax.all_to_all(chosen, ("z", "c"), 0, 0, tiled=True)
    rows = jnp.transpose(sent.reshape(NZ * NC, 2, 2, half), (1, 0, 2, 3)).reshape(2, 2 * NZ * NC, half)
    per = 2 * NZ * NC

    wg, wu, wd, rows = lax.optimization_barrier((gate_weight[0], up_weight[0], down_weight[0], rows))

    def join(own):
        other = z_swap(own)
        return jnp.where(
            parity == 0, jnp.concatenate([own, other], 0), jnp.concatenate([other, own], 0)
        )

    weight_in = jnp.concatenate([join(wg), join(wu)], axis=1)
    weight_down = join(wd)

    shared = lax.dot_general(
        selector, placed, (((0,), (0,)), ((), ())), preferred_element_type=F32
    ).astype(BF16)
    shared_other = core_swap(shared)
    pair = jnp.stack(
        [jnp.where(core == 0, shared, shared_other), jnp.where(core == 0, shared_other, shared)]
    ).reshape(NC, NZ, 2, NZ, 2)
    eye = jnp.eye(NC, dtype=BF16)
    mixing = pair[:, :, :, None, :, :] * eye[:, None, None, :, None, None]
    mixing = jnp.transpose(mixing, (1, 0, 2, 4, 3, 5)).reshape(per, per)
    row_gate = jnp.sum(jnp.where(jnp.eye(per, dtype=jnp.bool_), mixing, jnp.zeros((), BF16)), axis=1)
    row_gate = row_gate.astype(F32)
    prec = jnp.where(
        core == 0,
        precision.reshape(2, NC, block)[:, 0].reshape(1, half),
        precision.reshape(2, NC, block)[:, 1].reshape(1, half),
    )

    pieces = plane_gather(rows)
    pre = [
        jnp.dot(
            piece.reshape(RING * 2 * per, half), weight_in, preferred_element_type=F32
        ).reshape(RING, 2, per, 2 * hidden)
        for piece in pieces
    ]
    pre = core_sum(jnp.stack(pre))
    gate_pre, up_pre = pre[:, :, 0, :, :hidden], pre[:, :, 0, :, hidden:]
    gate_tan, up_tan = pre[:, :, 1, :, :hidden], pre[:, :, 1, :, hidden:]
    activated, derivative = sigmoid_parts(gate_pre)
    hidden_tan = (derivative * gate_tan * up_pre + activated * up_tan).astype(BF16)
    hidden_out = (activated * up_pre).astype(BF16)

    product = [
        lax.dot_general(
            hidden_tan[j].reshape(RING * per, hidden),
            weight_down,
            (((1,), (1,)), ((), ())),
            preferred_element_type=F32,
        ).astype(BF16).reshape(RING, per, half)
        for j in range(RING)
    ]
    summed = scatter_phase(product, False)
    summed = scatter_phase([summed[i] for i in range(RING)], True)

    x_rows = jnp.stack([piece[:, 0] for piece in pieces]).reshape(RING * RING * per, half)
    x_own = jnp.where(parity == 0, x_rows[:, :block], x_rows[:, block:])
    x_give = jnp.where(parity == 0, x_rows[:, block:], x_rows[:, :block])
    x_other = z_swap(x_give)

    returned = lax.all_to_all(summed, "z", 0, 0, tiled=True)
    combined = jnp.dot(mixing, returned, preferred_element_type=F32)
    cotangent = (prec * combined).astype(BF16)
    cot_rows = (row_gate[:, None] * cotangent.astype(F32)).astype(BF16)
    cot_sent = lax.all_to_all(cot_rows, "z", 0, 0, tiled=True)
    cot_pieces = plane_gather(cot_sent)
    back = [
        jnp.dot(
            piece.reshape(RING * per, half), weight_down, preferred_element_type=F32
        ).reshape(RING, per, hidden)
        for piece in cot_pieces
    ]
    back = core_sum(jnp.stack(back))
    gate_cot = (back * up_pre * derivative).astype(BF16)
    up_cot = (back * activated).astype(BF16)
    cots = jnp.concatenate([gate_cot, up_cot], axis=-1).reshape(RING * RING * per, 2 * hidden)
    cots_other = z_swap(cots)

    contract = (((0,), (0,)), ((), ()))
    c_rows = jnp.stack(cot_pieces).reshape(RING * RING * per, half)
    down_part = lax.dot_general(
        c_rows, hidden_out.reshape(RING * RING * per, hidden), contract, preferred_element_type=F32
    )
    down_own = jnp.where(parity == 0, down_part[:block], down_part[block:])
    down_give = jnp.where(parity == 0, down_part[block:], down_part[:block])
    down_other = z_swap(down_give.astype(BF16))
    grad_down = (down_own + down_other.astype(F32)).astype(BF16)

    grads = lax.dot_general(x_own, cots, contract, preferred_element_type=F32)
    grads = grads + lax.dot_general(x_other, cots_other, contract, preferred_element_type=F32)
    grad_gate = grads[:, :hidden].astype(BF16)
    grad_up = grads[:, hidden:].astype(BF16)
    return grad_gate[None], grad_up[None], grad_down[None]


def solution(mesh):
    fine = Mesh(mesh.devices.reshape(NX, NY, NZ, NC), ALL)
    rows = P(ALL, None)
    weights = P(("z", "c"), None, ("x", "y"))
    in_specs = (rows, rows, rows, rows, P(), weights, weights, weights)
    out_specs = (weights, weights, weights)
    return jax.shard_map(body, mesh=fine, in_specs=in_specs, out_specs=out_specs, check_vma=False)
```

time: 402 us -> 258 us (0.64); the launches traced: 401 us -> 253 us
  waiting for transfers between devices: 262 us -> 131 us
  starting transfers between devices: 13.3 us -> 52.6 us
  other arithmetic: 31.7 us -> 10.4 us
  matrix products: 32.7 us -> 19 us
  blocking collectives: 39.4 us -> 25.7 us
  between operations: 14 us -> 1.13 us
  local copies, waits for them, and re-layouts: 8.24 us -> 13.3 us
    reduce_scatter x1 -> x0, waiting for transfers between devices: 77.2 us -> none  [body(): lax.psum_scatter(product.astype(jnp.float32).astype(jnp.bfloat16), 'dp',...]
    all_gather x2 -> x0, waiting for transfers between devices: 48.9 us -> none  [deliver(): return lax.all_gather(exchanged, 'dp', axis=1, tiled=True)]
    ppermute x4 -> x27, starting transfers between devices: 3.63 us -> 45.6 us  [the longest x18 27.7 us: plane_shift(): return lax.ppermute(value, ('x', 'y', 'c'), pairs)]
    all_to_all x2 -> x1, blocking collectives: 39.4 us -> 25.7 us  [body(): sent = lax.all_to_all(chosen, ('z', 'c'), 0, 0, tiled=True)]
    dot_general x10 -> x19, matrix products: 32.7 us -> 19 us  [the longest x4 5.77 us: body(): lax.dot_general(hidden_tan[j].reshape(RING * per, hidden), weight_down, (...]
    ppermute x4 -> x27, waiting for transfers between devices: 125 us -> 116 us  [the longest x18 75.1 us: plane_shift(): return lax.ppermute(value, ('x', 'y', 'c'), pairs)]
    select_n x4 -> x6, other arithmetic: 10.5 us -> 2.18 us  [the longest x2 1.91 us: join(): jnp.where(parity == 0, jnp.concatenate([own, other], 0), jnp.concatenate(...]
    another operation x4 -> x6, other arithmetic: 9.27 us -> 1.95 us  [the longest x2 1.47 us: body(): jnp.stack([piece[:, 0] for piece in pieces])]
  transfers between devices with their start and end apart: 8 -> 29, of which waited for: 7 -> 21; matrix products, arithmetic and copies ran while one was open for 3% -> 10% of each run, Pallas kernels for 0% -> 0%
where the time goes in v1:
time: 258 us; the launch traced here: 253 us
  waiting for transfers between devices  131 us (51%)
  starting transfers between devices  52.6 us (20%)
  blocking collectives  25.7 us (10%)
  matrix products  19 us (7%)
  local copies, waits for them, and re-layouts  13.3 us (5%)
  other arithmetic  10.4 us (4%)
    ppermute x18, waiting for transfers between devices, plane_shift(): return lax.ppermute(value, ('x', 'y', 'c'), pairs)  75.1 us
    ppermute x6, waiting for transfers between devices, z_swap(): return lax.ppermute(value, 'z', [(z, z ^ 1) for z in range(NZ)])  39 us
    ppermute x18, starting transfers between devices, plane_shift(): return lax.ppermute(value, ('x', 'y', 'c'), pairs)  27.7 us
    all_to_all x1, blocking collectives, body(): sent = lax.all_to_all(chosen, ('z', 'c'), 0, 0, tiled=True)  25.7 us
    ppermute x3, starting transfers between devices, core_swap(): return lax.ppermute(value, 'c', [(0, 1), (1, 0)])  14.6 us
    all_to_all x1, waiting for transfers between devices, body(): returned = lax.all_to_all(summed, 'z', 0, 0, tiled=True)  7.74 us
    all_to_all x1, waiting for transfers between devices, body(): cot_sent = lax.all_to_all(cot_rows, 'z', 0, 0, tiled=True)  7.65 us
    dot_general x4, matrix products, body(): lax.dot_general(hidden_tan[j].reshape(RING * per, hidden), weight_down, (...  5.77 us
  transfers between devices with their start and end apart: 29, of which 21 were waited for; matrix products, arithmetic and copies ran while one was open for 10% of the time, Pallas kernels for 0%

profile of v1, /device:TPU:1, one launch (start us, length us, event | category | flops | bytes accessed | tf_op | source)
XLA Modules:
  0.0 253.2 jit_solution(7133920843962057131)
XLA Ops:
  1.6 2.7 %fusion = bf16[2,16,7168]{2,1,0:T(8,128)(2,1)S(1)} fusion(bf16[1,128,7168]{2,1,0:T(8,128)(2,1)} %bitcast.217, bf16[1,128,7168]{2,1,0:T(8,128)(2,1)} %bitcast.218, pred[128,16]{0,1:T(8,128)(4,1)S(1)} %bitcast.216, f32[128,16]{0,1:T(8,128)S(1)} %bitcast.215, f32[16]{0:T(128)S(1)} %eq.86), kind=kOutput, calls=%fused_computation.1 | convolution fusion | flops 60788736 | bytes 4139072 | tf_op jit(solution)/shard_map/tr,ktd->krd/dot_general | solution.py:84
  5.7 25.7 %all_to_all.33 = bf16[16,4,3584]{2,1,0:T(4,128)(2,1)S(1)} all-to-all(bf16[16,4,3584]{2,1,0:T(4,128)(2,1)S(1)} %copy.59), channel_id=1, replica_groups=mesh['x'=4,'y'=4,'z'=8,'c'=2] {'z','c'}, dimensions={0} | all-to-all | bytes 917504 | tf_op jit(solution)/shard_map/all_to_all | solution.py:87
  32.2 2.8 %collective-permute-start.2 = (bf16[2,32,3584]{2,1,0:T(8,128)(2,1)S(1)}, bf16[2,32,3584]{2,1,0:T(8,128)(2,1)S(1)}, u32[]{:S(2)}, u32[]{:S(2)}) collective-permute-start(bf16[2,32,3584]{2,1,0:T(8,128)(2,1)S(1)} %reshape.255), channel_id=1, source_target_pairs={{0,192},{1,49},{16,208},{17,1},{32,224},{33,17},{48,240},{49,33},{... | collective-permute-start | bytes 1376264 | tf_op jit(solution)/shard_map/ppermute | solution.py:30
  36.0 9.3 %collective-permute-done.2 = bf16[2,32,3584]{2,1,0:T(8,128)(2,1)S(1)} collective-permute-done((bf16[2,32,3584]{2,1,0:T(8,128)(2,1)S(1)}, bf16[2,32,3584]{2,1,0:T(8,128)(2,1)S(1)}, u32[]{:S(2)}, u32[]{:S(2)}) %collective-permute-start.2) | collective-permute-done | bytes 458784 | tf_op jit(solution)/shard_map/ppermute | solution.py:30
  45.3 3.4 %collective-permute-done = bf16[2,32,3584]{2,1,0:T(8,128)(2,1)S(1)} collective-permute-done((bf16[2,32,3584]{2,1,0:T(8,128)(2,1)S(1)}, bf16[2,32,3584]{2,1,0:T(8,128)(2,1)S(1)}, u32[]{:S(2)}, u32[]{:S(2)}) %collective-permute-start) | collective-permute-done | bytes 458784 | tf_op jit(solution)/shard_map/ppermute | solution.py:30
  52.1 2.5 collective-permute-start.4
  57.2 6.9 %collective-permute-done.7 = bf16[1792,128]{1,0:T(8,128)(2,1)} collective-permute-done((bf16[1792,128]{1,0:T(8,128)(2,1)}, bf16[1792,128]{1,0:T(8,128)(2,1)}, u32[]{:S(2)}, u32[]{:S(2)}) %collective-permute-start.7) | collective-permute-done | bytes 458784 | tf_op jit(solution)/shard_map/ppermute | solution.py:56
  65.7 8.2 %collective-permute-done.8 = bf16[1792,128]{1,0:T(8,128)(2,1)S(1)} collective-permute-done((bf16[1792,128]{1,0:T(8,128)(2,1)}, bf16[1792,128]{1,0:T(8,128)(2,1)S(1)}, u32[]{:S(2)}, u32[]{:S(2)}) %collective-permute-start.8) | collective-permute-done | bytes 458784 | tf_op jit(solution)/shard_map/ppermute | solution.py:56
  74.8 2.2 fusion.25
  77.0 18.4 %collective-permute-done.4 = bf16[4,2,32,3584]{3,2,0,1:T(8,128)(2,1)} collective-permute-done((bf16[4,2,32,3584]{3,2,0,1:T(8,128)(2,1)}, bf16[4,2,32,3584]{3,2,0,1:T(8,128)(2,1)}, u32[]{:S(2)}, u32[]{:S(2)}) %collective-permute-start.4) | collective-permute-done | bytes 1835040 | tf_op jit(solution)/shard_map/ppermute | solution.py:30
  95.5 2.2 fusion.28
  104.5 9.3 %collective-permute-done.10 = bf16[1792,128]{1,0:T(8,128)(2,1)S(1)} collective-permute-done((bf16[1792,128]{1,0:T(8,128)(2,1)}, bf16[1792,128]{1,0:T(8,128)(2,1)S(1)}, u32[]{:S(2)}, u32[]{:S(2)}) %collective-permute-start.10) | collective-permute-done | bytes 458784 | tf_op jit(solution)/shard_map/ppermute | solution.py:56
  123.1 4.9 %collective-permute-done.11 = bf16[4,32,3584]{2,1,0:T(8,128)(2,1)} collective-permute-done((bf16[4,32,3584]{2,1,0:T(8,128)(2,1)}, bf16[4,32,3584]{2,1,0:T(8,128)(2,1)}, u32[]{:S(2)}, u32[]{:S(2)}) %collective-permute-start.11) | collective-permute-done | bytes 917536 | tf_op jit(solution)/shard_map/ppermute | solution.py:30
  128.0 12.7 %collective-permute-done.13 = bf16[4,32,3584]{2,1,0:T(8,128)(2,1)} collective-permute-done((bf16[4,32,3584]{2,1,0:T(8,128)(2,1)}, bf16[4,32,3584]{2,1,0:T(8,128)(2,1)}, u32[]{:S(2)}, u32[]{:S(2)}) %collective-permute-start.13) | collective-permute-done | bytes 917536 | tf_op jit(solution)/shard_map/ppermute | solution.py:30
  140.7 2.2 add_convert_fusion
  143.1 2.7 %collective-permute-start.15 = (bf16[32,3584]{1,0:T(8,128)(2,1)S(1)}, bf16[32,3584]{1,0:T(8,128)(2,1)S(1)}, u32[]{:S(2)}, u32[]{:S(2)}) collective-permute-start(bf16[32,3584]{1,0:T(8,128)(2,1)S(1)} %get-tuple-element.54), channel_id=1, source_target_pairs={{0,128},{1,33},{16,144},{17,49},{32,160},{33,1},{48,176},{49,17},{... | collective-permute-start | bytes 688136 | tf_op jit(solution)/shard_map/ppermute | solution.py:30
  145.8 2.0 collective-permute-start.14
  149.2 2.4 collective-permute-done.15
  153.4 3.6 %all-to-all-start.1 = ((bf16[8,4,3584]{2,1,0:T(4,128)(2,1)}), bf16[8,4,3584]{2,1,0:T(4,128)(2,1)S(1)}, u32[]{:S(2)}, u32[]{:S(2)}) async-start(bf16[8,4,3584]{2,1,0:T(4,128)(2,1)} %all_to_all.24), calls=%async_computation.1 | async-start | bytes 458752 | tf_op jit(solution)/shard_map/all_to_all | solution.py:151
  158.2 7.7 %all-to-all-done.1 = bf16[8,4,3584]{2,1,0:T(4,128)(2,1)S(1)} async-done(((bf16[8,4,3584]{2,1,0:T(4,128)(2,1)}), bf16[8,4,3584]{2,1,0:T(4,128)(2,1)S(1)}, u32[]{:S(2)}, u32[]{:S(2)}) %all-to-all-start.1) | async-done | bytes 229408 | tf_op jit(solution)/shard_map/all_to_all | solution.py:151
  167.0 3.4 %all-to-all-start.2 = ((bf16[8,4,3584]{2,1,0:T(4,128)(2,1)}), bf16[8,4,3584]{2,1,0:T(4,128)(2,1)S(1)}, u32[]{:S(2)}, u32[]{:S(2)}) async-start(bf16[8,4,3584]{2,1,0:T(4,128)(2,1)} %all_to_all.27), calls=%async_computation.2 | async-start | bytes 458752 | tf_op jit(solution)/shard_map/all_to_all | solution.py:155
  171.7 7.7 %all-to-all-done.2 = bf16[8,4,3584]{2,1,0:T(4,128)(2,1)S(1)} async-done(((bf16[8,4,3584]{2,1,0:T(4,128)(2,1)}), bf16[8,4,3584]{2,1,0:T(4,128)(2,1)S(1)}, u32[]{:S(2)}, u32[]{:S(2)}) %all-to-all-start.2) | async-done | bytes 229408 | tf_op jit(solution)/shard_map/all_to_all | solution.py:155
  179.4 3.4 %collective-permute-start.19 = (bf16[32,3584]{1,0:T(8,128)(2,1)S(1)}, bf16[32,3584]{1,0:T(8,128)(2,1)S(1)}, u32[]{:S(2)}, u32[]{:S(2)}) collective-permute-start(bf16[32,3584]{1,0:T(8,128)(2,1)S(1)} %all_to_all.29), channel_id=1, source_target_pairs={{0,192},{1,49},{16,208},{17,1},{32,224},{33,17},{48,240},{49,33},{... | collective-permute-start | bytes 688136 | tf_op jit(solution)/shard_map/ppermute | solution.py:30
  184.7 3.5 %collective-permute-done.19 = bf16[32,3584]{1,0:T(8,128)(2,1)S(1)} collective-permute-done((bf16[32,3584]{1,0:T(8,128)(2,1)S(1)}, bf16[32,3584]{1,0:T(8,128)(2,1)S(1)}, u32[]{:S(2)}, u32[]{:S(2)}) %collective-permute-start.19) | collective-permute-done | bytes 229408 | tf_op jit(solution)/shard_map/ppermute | solution.py:30
  189.3 2.4 collective-permute-done.17
  191.8 5.5 %collective-permute-start.21 = (bf16[4,32,3584]{2,1,0:T(8,128)(2,1)S(1)}, bf16[4,32,3584]{2,1,0:T(8,128)(2,1)S(1)}, u32[]{:S(2)}, u32[]{:S(2)}) collective-permute-start(bf16[4,32,3584]{2,1,0:T(8,128)(2,1)S(1)} %get-tuple-element.50), channel_id=1, source_target_pairs={{0,32},{1,129},{16,48},{17,145},{32,0},{33,161},{48,16},{49,177},{... | collective-permute-start | bytes 2752520 | tf_op jit(solution)/shard_map/ppermute | solution.py:30
  197.9 2.7 %collective-permute-start.22 = (bf16[4,32,3584]{2,1,0:T(8,128)(2,1)S(1)}, bf16[4,32,3584]{2,1,0:T(8,128)(2,1)S(1)}, u32[]{:S(2)}, u32[]{:S(2)}) collective-permute-start(bf16[4,32,3584]{2,1,0:T(8,128)(2,1)S(1)} %get-tuple-element.50), channel_id=1, source_target_pairs={{0,48},{1,193},{16,0},{17,209},{32,16},{33,225},{48,32},{49,241},{... | collective-permute-start | bytes 2752520 | tf_op jit(solution)/shard_map/ppermute | solution.py:30
  202.2 6.1 %collective-permute-done.21 = bf16[4,32,3584]{2,1,0:T(8,128)(2,1)S(1)} collective-permute-done((bf16[4,32,3584]{2,1,0:T(8,128)(2,1)S(1)}, bf16[4,32,3584]{2,1,0:T(8,128)(2,1)S(1)}, u32[]{:S(2)}, u32[]{:S(2)}) %collective-permute-start.21) | collective-permute-done | bytes 917536 | tf_op jit(solution)/shard_map/ppermute | solution.py:30
  208.7 9.6 %collective-permute-done.20 = bf16[4,32,3584]{2,1,0:T(8,128)(2,1)S(1)} collective-permute-done((bf16[4,32,3584]{2,1,0:T(8,128)(2,1)S(1)}, bf16[4,32,3584]{2,1,0:T(8,128)(2,1)S(1)}, u32[]{:S(2)}, u32[]{:S(2)}) %collective-permute-start.20) | collective-permute-done | bytes 917536 | tf_op jit(solution)/shard_map/ppermute | solution.py:30
  219.1 12.7 %collective-permute-start.23 = (f32[4,4,32,128]{3,2,0,1:T(8,128)S(1)}, f32[4,4,32,128]{3,2,0,1:T(8,128)S(1)}, u32[]{:S(2)}, u32[]{:S(2)}) collective-permute-start(f32[4,4,32,128]{3,2,0,1:T(8,128)S(1)} %pad_maximum_fusion.4), channel_id=1, source_target_pairs={{0,1},{1,0},{2,3},{3,2},{4,5},{5,4},{6,7},{7,6},{8,9},{9,8},{10,11... | collective-permute-start | bytes 786440 | tf_op jit(solution)/shard_map/ppermute | solution.py:52
  235.8 10.1 %collective-permute-done.26 = bf16[1792,128]{1,0:T(8,128)(2,1)S(1)} collective-permute-done((bf16[1792,128]{1,0:T(8,128)(2,1)S(1)}, bf16[1792,128]{1,0:T(8,128)(2,1)S(1)}, u32[]{:S(2)}, u32[]{:S(2)}) %collective-permute-start.26) | collective-permute-done | bytes 458784 | tf_op jit(solution)/shard_map/ppermute | solution.py:56
  246.8 4.7 %collective-permute-done.25 = bf16[512,256]{1,0:T(8,128)(2,1)S(1)} collective-permute-done((bf16[512,256]{1,0:T(8,128)(2,1)S(1)}, bf16[512,256]{1,0:T(8,128)(2,1)S(1)}, u32[]{:S(2)}, u32[]{:S(2)}) %collective-permute-start.25) | collective-permute-done | bytes 262176 | tf_op jit(solution)/shard_map/ppermute | solution.py:56
  (140 shorter events, 48.7 us)
Async XLA Ops:
  32.2 13.2 %collective-permute-start.2 = (bf16[2,32,3584]{2,1,0:T(8,128)(2,1)S(1)}, bf16[2,32,3584]{2,1,0:T(8,128)(2,1)S(1)}, u32[]{:S(2)}, u32[]{:S(2)}) collective-permute-start(bf16[2,32,3584]{2,1,0:T(8,128)(2,1)S(1)} %reshape.255), channel_id=1, source_target_pairs={{0,192},{1,49},{16,208},{17,1},{32,224},{33,17},{48,240},{49,33},{... | collective-permute-start | bytes 1376264 | tf_op jit(solution)/shard_map/ppermute | solution.py:30
  35.0 10.3 %collective-permute-start.1 = (bf16[2,32,3584]{2,1,0:T(8,128)(2,1)S(1)}, bf16[2,32,3584]{2,1,0:T(8,128)(2,1)S(1)}, u32[]{:S(2)}, u32[]{:S(2)}) collective-permute-start(bf16[2,32,3584]{2,1,0:T(8,128)(2,1)S(1)} %reshape.255), channel_id=1, source_target_pairs={{0,128},{1,33},{16,144},{17,49},{32,160},{33,1},{48,176},{49,17},{... | collective-permute-start | bytes 1376264 | tf_op jit(solution)/shard_map/ppermute | solution.py:30
  35.3 13.4 %collective-permute-start = (bf16[2,32,3584]{2,1,0:T(8,128)(2,1)S(1)}, bf16[2,32,3584]{2,1,0:T(8,128)(2,1)S(1)}, u32[]{:S(2)}, u32[]{:S(2)}) collective-permute-start(bf16[2,32,3584]{2,1,0:T(8,128)(2,1)S(1)} %reshape.255), channel_id=1, source_target_pairs={{0,64},{1,17},{16,80},{17,33},{32,96},{33,49},{48,112},{49,1},{64,... | collective-permute-start | bytes 1376264 | tf_op jit(solution)/shard_map/ppermute | solution.py:30
  50.9 23.9 %collective-permute-start.3 = (bf16[4,2,32,3584]{3,2,0,1:T(8,128)(2,1)}, bf16[4,2,32,3584]{3,2,0,1:T(8,128)(2,1)}, u32[]{:S(2)}, u32[]{:S(2)}) collective-permute-start(bf16[4,2,32,3584]{3,2,0,1:T(8,128)(2,1)} %copy.62), channel_id=1, source_target_pairs={{0,16},{1,65},{16,32},{17,81},{32,48},{33,97},{48,0},{49,113},{64,... | collective-permute-start | bytes 5505032 | tf_op jit(solution)/shard_map/ppermute | solution.py:30
  52.1 11.9 %collective-permute-start.7 = (bf16[1792,128]{1,0:T(8,128)(2,1)}, bf16[1792,128]{1,0:T(8,128)(2,1)}, u32[]{:S(2)}, u32[]{:S(2)}) collective-permute-start(bf16[1792,128]{1,0:T(8,128)(2,1)} %bitcast), channel_id=1, source_target_pairs={{0,2},{2,0},{4,6},{6,4},{8,10},{10,8},{12,14},{14,12},{1,3},{3,1},... | collective-permute-start | bytes 1376264 | tf_op jit(solution)/shard_map/ppermute | solution.py:56
  52.1 43.3 %collective-permute-start.4 = (bf16[4,2,32,3584]{3,2,0,1:T(8,128)(2,1)}, bf16[4,2,32,3584]{3,2,0,1:T(8,128)(2,1)}, u32[]{:S(2)}, u32[]{:S(2)}) collective-permute-start(bf16[4,2,32,3584]{3,2,0,1:T(8,128)(2,1)} %copy.62), channel_id=1, source_target_pairs={{0,32},{1,129},{16,48},{17,145},{32,0},{33,161},{48,16},{49,177},{... | collective-permute-start | bytes 5505032 | tf_op jit(solution)/shard_map/ppermute | solution.py:30
  54.6 19.3 %copy-start.9 = (bf16[1,1792,128]{2,1,0:T(8,128)(2,1)S(1)}, bf16[1,1792,128]{2,1,0:T(8,128)(2,1)}, u32[]{:S(2)}) copy-start(bf16[1,1792,128]{2,1,0:T(8,128)(2,1)} %param.14) | copy-start | bytes 1376260
  54.6 19.6 %copy-start.2 = (bf16[2,32,3584]{2,1,0:T(8,128)(2,1)S(1)}, bf16[2,32,3584]{2,1,0:T(8,128)(2,1)}, u32[]{:S(2)}) copy-start(bf16[2,32,3584]{2,1,0:T(8,128)(2,1)} %copy-done.1) | copy-start | bytes 1376260
  54.6 19.3 %collective-permute-start.8 = (bf16[1792,128]{1,0:T(8,128)(2,1)}, bf16[1792,128]{1,0:T(8,128)(2,1)S(1)}, u32[]{:S(2)}, u32[]{:S(2)}) collective-permute-start(bf16[1792,128]{1,0:T(8,128)(2,1)} %bitcast.199), channel_id=1, source_target_pairs={{0,2},{2,0},{4,6},{6,4},{8,10},{10,8},{12,14},{14,12},{1,3},{3,1},... | collective-permute-start | bytes 1376264 | tf_op jit(solution)/shard_map/ppermute | solution.py:56
  56.1 41.6 %collective-permute-start.5 = (bf16[4,2,32,3584]{3,2,1,0:T(8,128)(2,1)S(1)}, bf16[4,2,32,3584]{3,2,1,0:T(8,128)(2,1)S(1)}, u32[]{:S(2)}, u32[]{:S(2)}) collective-permute-start(bf16[4,2,32,3584]{3,2,1,0:T(8,128)(2,1)S(1)} %pad_maximum_fusion.1), channel_id=1, source_target_pairs={{0,48},{1,193},{16,0},{17,209},{32,16},{33,225},{48,32},{49,241},{... | collective-permute-start | bytes 5505032 | tf_op jit(solution)/shard_map/ppermute | solution.py:30
  77.0 21.3 %copy-start.4 = (f32[1,4,2,32,256]{4,3,2,1,0:T(8,128)}, f32[1,4,2,32,256]{4,3,2,1,0:T(8,128)S(1)}, u32[]{:S(2)}) copy-start(f32[1,4,2,32,256]{4,3,2,1,0:T(8,128)S(1)} %fusion.25) | copy-start | bytes 786436
  99.2 3.7 %collective-permute-start.9 = (f32[4,4,2,32,256]{4,3,2,0,1:T(8,128)S(1)}, f32[4,4,2,32,256]{4,3,2,0,1:T(8,128)}, u32[]{:S(2)}, u32[]{:S(2)}) collective-permute-start(f32[4,4,2,32,256]{4,3,2,0,1:T(8,128)S(1)} %copy.70), channel_id=1, source_target_pairs={{0,1},{1,0},{2,3},{3,2},{4,5},{5,4},{6,7},{7,6},{8,9},{9,8},{10,11... | collective-permute-start | bytes 3145736 | tf_op jit(solution)/shard_map/ppermute | solution.py:52
  100.7 19.2 %collective-permute-start.6 = (bf16[16,16]{1,0:T(8,128)(2,1)S(1)}, bf16[16,16]{1,0:T(8,128)(2,1)S(1)}, u32[]{:S(2)}, u32[]{:S(2)}) collective-permute-start(bf16[16,16]{1,0:T(8,128)(2,1)S(1)} %convolution_convert_fusion.5), channel_id=1, source_target_pairs={{0,1},{1,0},{2,3},{3,2},{4,5},{5,4},{6,7},{7,6},{8,9},{9,8},{10,11... | collective-permute-start | bytes 1544 | tf_op jit(solution)/shard_map/ppermute | solution.py:52
  101.3 12.4 %collective-permute-start.10 = (bf16[1792,128]{1,0:T(8,128)(2,1)}, bf16[1792,128]{1,0:T(8,128)(2,1)S(1)}, u32[]{:S(2)}, u32[]{:S(2)}) collective-permute-start(bf16[1792,128]{1,0:T(8,128)(2,1)} %bitcast.222), channel_id=1, source_target_pairs={{0,2},{2,0},{4,6},{6,4},{8,10},{10,8},{12,14},{14,12},{1,3},{3,1},... | collective-permute-start | bytes 1376264 | tf_op jit(solution)/shard_map/ppermute | solution.py:56
  115.1 12.9 %collective-permute-start.11 = (bf16[4,32,3584]{2,1,0:T(8,128)(2,1)}, bf16[4,32,3584]{2,1,0:T(8,128)(2,1)}, u32[]{:S(2)}, u32[]{:S(2)}) collective-permute-start(bf16[4,32,3584]{2,1,0:T(8,128)(2,1)} %bitcast.40), channel_id=1, source_target_pairs={{0,48},{1,193},{16,0},{17,209},{32,16},{33,225},{48,32},{49,241},{... | collective-permute-start | bytes 2752520 | tf_op jit(solution)/shard_map/ppermute | solution.py:30
  116.8 23.9 %collective-permute-start.13 = (bf16[4,32,3584]{2,1,0:T(8,128)(2,1)}, bf16[4,32,3584]{2,1,0:T(8,128)(2,1)}, u32[]{:S(2)}, u32[]{:S(2)}) collective-permute-start(bf16[4,32,3584]{2,1,0:T(8,128)(2,1)} %bitcast.44), channel_id=1, source_target_pairs={{0,16},{1,65},{16,32},{17,81},{32,48},{33,97},{48,0},{49,113},{64,... | collective-permute-start | bytes 2752520 | tf_op jit(solution)/shard_map/ppermute | solution.py:30
  119.3 21.4 %collective-permute-start.12 = (bf16[4,32,3584]{2,1,0:T(8,128)(2,1)}, bf16[4,32,3584]{2,1,0:T(8,128)(2,1)}, u32[]{:S(2)}, u32[]{:S(2)}) collective-permute-start(bf16[4,32,3584]{2,1,0:T(8,128)(2,1)} %bitcast.42), channel_id=1, source_target_pairs={{0,32},{1,129},{16,48},{17,145},{32,0},{33,161},{48,16},{49,177},{... | collective-permute-start | bytes 2752520 | tf_op jit(solution)/shard_map/ppermute | solution.py:30
  143.0 6.2 %collective-permute-start.16 = (bf16[32,3584]{1,0:T(8,128)(2,1)S(1)}, bf16[32,3584]{1,0:T(8,128)(2,1)S(1)}, u32[]{:S(2)}, u32[]{:S(2)}) collective-permute-start(bf16[32,3584]{1,0:T(8,128)(2,1)S(1)} %get-tuple-element.53), channel_id=1, source_target_pairs={{0,64},{1,17},{16,80},{17,33},{32,96},{33,49},{48,112},{49,1},{64,... | collective-permute-start | bytes 688136 | tf_op jit(solution)/shard_map/ppermute | solution.py:30
  143.1 8.5 %collective-permute-start.15 = (bf16[32,3584]{1,0:T(8,128)(2,1)S(1)}, bf16[32,3584]{1,0:T(8,128)(2,1)S(1)}, u32[]{:S(2)}, u32[]{:S(2)}) collective-permute-start(bf16[32,3584]{1,0:T(8,128)(2,1)S(1)} %get-tuple-element.54), channel_id=1, source_target_pairs={{0,128},{1,33},{16,144},{17,49},{32,160},{33,1},{48,176},{49,17},{... | collective-permute-start | bytes 688136 | tf_op jit(solution)/shard_map/ppermute | solution.py:30
  145.8 6.7 %collective-permute-start.14 = (bf16[32,3584]{1,0:T(8,128)(2,1)S(1)}, bf16[32,3584]{1,0:T(8,128)(2,1)S(1)}, u32[]{:S(2)}, u32[]{:S(2)}) collective-permute-start(bf16[32,3584]{1,0:T(8,128)(2,1)S(1)} %get-tuple-element.55), channel_id=1, source_target_pairs={{0,192},{1,49},{16,208},{17,1},{32,224},{33,17},{48,240},{49,33},{... | collective-permute-start | bytes 688136 | tf_op jit(solution)/shard_map/ppermute | solution.py:30
  153.4 12.6 %all-to-all-start.1 = ((bf16[8,4,3584]{2,1,0:T(4,128)(2,1)}), bf16[8,4,3584]{2,1,0:T(4,128)(2,1)S(1)}, u32[]{:S(2)}, u32[]{:S(2)}) async-start(bf16[8,4,3584]{2,1,0:T(4,128)(2,1)} %all_to_all.24), calls=%async_computation.1 | async-start | bytes 458752 | tf_op jit(solution)/shard_map/all_to_all | solution.py:151
  167.0 12.3 %all-to-all-start.2 = ((bf16[8,4,3584]{2,1,0:T(4,128)(2,1)}), bf16[8,4,3584]{2,1,0:T(4,128)(2,1)S(1)}, u32[]{:S(2)}, u32[]{:S(2)}) async-start(bf16[8,4,3584]{2,1,0:T(4,128)(2,1)} %all_to_all.27), calls=%async_computation.2 | async-start | bytes 458752 | tf_op jit(solution)/shard_map/all_to_all | solution.py:155
  179.4 8.8 %collective-permute-start.19 = (bf16[32,3584]{1,0:T(8,128)(2,1)S(1)}, bf16[32,3584]{1,0:T(8,128)(2,1)S(1)}, u32[]{:S(2)}, u32[]{:S(2)}) collective-permute-start(bf16[32,3584]{1,0:T(8,128)(2,1)S(1)} %all_to_all.29), channel_id=1, source_target_pairs={{0,192},{1,49},{16,208},{17,1},{32,224},{33,17},{48,240},{49,33},{... | collective-permute-start | bytes 688136 | tf_op jit(solution)/shard_map/ppermute | solution.py:30
  182.8 6.5 %collective-permute-start.18 = (bf16[32,3584]{1,0:T(8,128)(2,1)S(1)}, bf16[32,3584]{1,0:T(8,128)(2,1)S(1)}, u32[]{:S(2)}, u32[]{:S(2)}) collective-permute-start(bf16[32,3584]{1,0:T(8,128)(2,1)S(1)} %all_to_all.29), channel_id=1, source_target_pairs={{0,128},{1,33},{16,144},{17,49},{32,160},{33,1},{48,176},{49,17},{... | collective-permute-start | bytes 688136 | tf_op jit(solution)/shard_map/ppermute | solution.py:30
  183.4 8.2 %collective-permute-start.17 = (bf16[32,3584]{1,0:T(8,128)(2,1)S(1)}, bf16[32,3584]{1,0:T(8,128)(2,1)S(1)}, u32[]{:S(2)}, u32[]{:S(2)}) collective-permute-start(bf16[32,3584]{1,0:T(8,128)(2,1)S(1)} %all_to_all.29), channel_id=1, source_target_pairs={{0,64},{1,17},{16,80},{17,33},{32,96},{33,49},{48,112},{49,1},{64,... | collective-permute-start | bytes 688136 | tf_op jit(solution)/shard_map/ppermute | solution.py:30
  191.8 16.5 %collective-permute-start.21 = (bf16[4,32,3584]{2,1,0:T(8,128)(2,1)S(1)}, bf16[4,32,3584]{2,1,0:T(8,128)(2,1)S(1)}, u32[]{:S(2)}, u32[]{:S(2)}) collective-permute-start(bf16[4,32,3584]{2,1,0:T(8,128)(2,1)S(1)} %get-tuple-element.50), channel_id=1, source_target_pairs={{0,32},{1,129},{16,48},{17,145},{32,0},{33,161},{48,16},{49,177},{... | collective-permute-start | bytes 2752520 | tf_op jit(solution)/shard_map/ppermute | solution.py:30
  197.8 20.5 %collective-permute-start.20 = (bf16[4,32,3584]{2,1,0:T(8,128)(2,1)S(1)}, bf16[4,32,3584]{2,1,0:T(8,128)(2,1)S(1)}, u32[]{:S(2)}, u32[]{:S(2)}) collective-permute-start(bf16[4,32,3584]{2,1,0:T(8,128)(2,1)S(1)} %get-tuple-element.50), channel_id=1, source_target_pairs={{0,16},{1,65},{16,32},{17,81},{32,48},{33,97},{48,0},{49,113},{64,... | collective-permute-start | bytes 2752520 | tf_op jit(solution)/shard_map/ppermute | solution.py:30
  197.9 20.8 %collective-permute-start.22 = (bf16[4,32,3584]{2,1,0:T(8,128)(2,1)S(1)}, bf16[4,32,3584]{2,1,0:T(8,128)(2,1)S(1)}, u32[]{:S(2)}, u32[]{:S(2)}) collective-permute-start(bf16[4,32,3584]{2,1,0:T(8,128)(2,1)S(1)} %get-tuple-element.50), channel_id=1, source_target_pairs={{0,48},{1,193},{16,0},{17,209},{32,16},{33,225},{48,32},{49,241},{... | collective-permute-start | bytes 2752520 | tf_op jit(solution)/shard_map/ppermute | solution.py:30
  200.7 46.1 %collective-permute-start.24 = (bf16[512,1792]{1,0:T(8,128)(2,1)S(1)}, bf16[512,1792]{1,0:T(8,128)(2,1)S(1)}, u32[]{:S(2)}, u32[]{:S(2)}) collective-permute-start(bf16[512,1792]{1,0:T(8,128)(2,1)S(1)} %broadcast_select_fusion), channel_id=1, source_target_pairs={{0,2},{2,0},{4,6},{6,4},{8,10},{10,8},{12,14},{14,12},{1,3},{3,1},... | collective-permute-start | bytes 5505032 | tf_op jit(solution)/shard_map/ppermute | solution.py:56
  219.1 14.2 %collective-permute-start.23 = (f32[4,4,32,128]{3,2,0,1:T(8,128)S(1)}, f32[4,4,32,128]{3,2,0,1:T(8,128)S(1)}, u32[]{:S(2)}, u32[]{:S(2)}) collective-permute-start(f32[4,4,32,128]{3,2,0,1:T(8,128)S(1)} %pad_maximum_fusion.4), channel_id=1, source_target_pairs={{0,1},{1,0},{2,3},{3,2},{4,5},{5,4},{6,7},{7,6},{8,9},{9,8},{10,11... | collective-permute-start | bytes 786440 | tf_op jit(solution)/shard_map/ppermute | solution.py:52
  233.2 12.7 %collective-permute-start.26 = (bf16[1792,128]{1,0:T(8,128)(2,1)S(1)}, bf16[1792,128]{1,0:T(8,128)(2,1)S(1)}, u32[]{:S(2)}, u32[]{:S(2)}) collective-permute-start(bf16[1792,128]{1,0:T(8,128)(2,1)S(1)} %select_convert_fusion), channel_id=1, source_target_pairs={{0,2},{2,0},{4,6},{6,4},{8,10},{10,8},{12,14},{14,12},{1,3},{3,1},... | collective-permute-start | bytes 1376264 | tf_op jit(solution)/shard_map/ppermute | solution.py:56
  233.6 18.0 %collective-permute-start.25 = (bf16[512,256]{1,0:T(8,128)(2,1)S(1)}, bf16[512,256]{1,0:T(8,128)(2,1)S(1)}, u32[]{:S(2)}, u32[]{:S(2)}) collective-permute-start(bf16[512,256]{1,0:T(8,128)(2,1)S(1)} %bitcast.201), channel_id=1, source_target_pairs={{0,2},{2,0},{4,6},{6,4},{8,10},{10,8},{12,14},{14,12},{1,3},{3,1},... | collective-permute-start | bytes 786440 | tf_op jit(solution)/shard_map/ppermute | solution.py:56
  (15 other events, 56.8 us)
